TPU v7x, 32 devices: a whole 2x2x4 slice. The times are simulated.
32 devices in a mesh: grp: 2 (over x), blk: 16 (over z, y, core).
Axes of the slice: x: 2, y: 2, z: 4, core: 2. Of those that a mesh axis runs over, the one named last changes fastest.
Arguments:
- tokens_act: bfloat16 [512, 8192], P(('grp', 'blk')), parts along dimension 0, may hold values from -6 to 6
- tokens_grad: bfloat16 [512, 28672], P(('grp', 'blk')), parts along dimension 0, may hold values from -6 to 6
- act_factors: bfloat16 [8192, 6144], P(None, ('grp', 'blk')), parts along dimension 1, may hold values from -0.0068359375 to 0.0068359375
- grad_factors: bfloat16 [28672, 6144], P(None, ('grp', 'blk')), parts along dimension 1, may hold values from -0.0034179688 to 0.0034179688
- act_eigen: float32 [8192], replicated, may hold values from 0.1 to 10
- grad_eigen: float32 [28672], replicated, may hold values from 0.1 to 10
- doc_lengths: int32 [32], P('grp'), parts along dimension 0, may hold values from 1 to 32, 256 in all
Outputs:
- scores: float32 [192, 16], P(('grp', 'blk')), parts along dimension 0
There are 2 independent parts, one for each index of `grp`. A program takes and returns all parts, laid end to end along the dimension named above; an argument that names none is the same for every part. Nothing has to cross between parts.
Inputs may be any that keep to these rules, and one draw needn't show every extreme that they name: `doc_lengths`: the counts sum to 256.
All inputs are finite; a program needn't handle non-finite values.
Results may differ from a plain program's by a relative error of at most 0.0041.
Values may be sent and summed in bfloat16 or wider, within the bound.
A program may use at most 128 MiB of HBM per device.

v0:
```python
import jax
import jax.numpy as jnp
from jax import lax
from jax.sharding import PartitionSpec as P

RANK = 32


def from_behind(value, axis, steps):
    count = lax.axis_size(axis)
    pairs = [(source, (source + steps) % count) for source in range(count)]
    return lax.ppermute(value, axis, pairs)


def precondition(factors, eigen):
    damping = 0.1 * jnp.mean(eigen)
    return (factors.astype(jnp.float32) / (eigen + damping)[:, None]).astype(jnp.bfloat16)


def local(tokens_act, tokens_grad, act_factors, grad_factors, act_eigen, grad_eigen, doc_lengths):
    act_pre = precondition(act_factors, act_eigen)
    grad_pre = precondition(grad_factors, grad_eigen)
    tok_local = tokens_act.shape[0]
    query_local = act_pre.shape[1] // RANK
    cycle_size = lax.axis_size("blk")
    position = lax.axis_index("blk")
    doc_ends = jnp.cumsum(doc_lengths)
    doc_starts = doc_ends - doc_lengths
    local_rows = jnp.arange(tok_local, dtype=jnp.int32)

    def add_scores(totals, act_proj, grad_proj, token_index, live_rows):
        per_token = (act_proj * grad_proj).reshape(act_proj.shape[0], query_local, RANK).sum(axis=2)
        member = (
            (token_index[None, :] >= doc_starts[:, None])
            & (token_index[None, :] < doc_ends[:, None])
        ).astype(jnp.float32)
        member = member * live_rows[None, :]
        return totals + jnp.dot(
            member, per_token, precision=lax.Precision.HIGHEST, preferred_element_type=jnp.float32
        )

    def accumulate(totals, act_rows, grad_rows, token_index, live_rows):
        act_proj = jnp.dot(act_rows, act_pre, preferred_element_type=jnp.float32)
        grad_proj = jnp.dot(grad_rows, grad_pre, preferred_element_type=jnp.float32)
        return add_scores(totals, act_proj, grad_proj, token_index, live_rows)

    initial = jnp.zeros((doc_lengths.shape[0], query_local), jnp.float32)
    all_live = jnp.ones((tok_local,), jnp.float32)
    totals = accumulate(
        initial, tokens_act, tokens_grad, position * tok_local + local_rows, all_live
    )

    def cycle_turn(offset, carry):
        totals, act_rows, grad_rows = carry
        act_rows, grad_rows = from_behind((act_rows, grad_rows), "blk", 1)
        source = (position - offset) % cycle_size
        totals = accumulate(totals, act_rows, grad_rows, source * tok_local + local_rows, all_live)
        return (totals, act_rows, grad_rows)

    totals, _, _ = lax.fori_loop(1, cycle_size, cycle_turn, (totals, tokens_act, tokens_grad))
    return totals.T


def solution(mesh):
    placed = (
        P(("grp", "blk"), None),
        P(("grp", "blk"), None),
        P(None, ("grp", "blk")),
        P(None, ("grp", "blk")),
        P(),
        P(),
        P("grp"),
    )
    return jax.shard_map(
        local, mesh=mesh, in_specs=placed, out_specs=P(("grp", "blk"), None), check_vma=False
    )
```

profile of v0, /device:TPU:0, one launch (start us, length us, event | category | flops | bytes accessed | tf_op | source)
XLA Modules:
  0.0 456.0 jit_solution(16525880326990162321)
XLA Ops:
  0.0 0.9 copy.28
  1.0 1.2 copy.29
  2.1 5.9 %copy.12 = bf16[8192,192]{1,0:T(8,128)(2,1)} copy(bf16[8192,192]{0,1:T(8,128)(2,1)} %param.11) | data formatting | bytes 6291456 | tf_op args[2]
  8.0 1.4 reduce_sum.43
  10.1 0.8 broadcast_add_fusion.1
  10.8 2.9 divide_convert_fusion.1
  13.7 2.0 copy-done.1
  15.7 0.7 fusion.17
  16.3 16.8 %copy.13 = bf16[28672,192]{1,0:T(8,128)(2,1)} copy(bf16[28672,192]{0,1:T(8,128)(2,1)} %param.12) | data formatting | bytes 22020096 | tf_op args[3]
  33.1 0.6 reduce_sum.44
  34.4 9.0 %divide_convert_fusion = bf16[28672,192]{1,0:T(8,128)(2,1)S(1)} fusion(bf16[28672,192]{1,0:T(8,128)(2,1)} %copy.13, f32[28672]{0:T(1024)S(1)} %broadcast_add_fusion), kind=kLoop, calls=%fused_computation.10 | loop fusion | flops 16515072 | bytes 22134784 | tf_op jit(solution)/shard_map/convert_element_type | solution.py:17
  43.4 5.2 %copy-done = bf16[28672,192]{1,0:T(8,128)(2,1)} copy-done((bf16[28672,192]{1,0:T(8,128)(2,1)}, bf16[28672,192]{1,0:T(8,128)(2,1)S(1)}, u32[]{:S(2)}) %copy-start) | copy-done | bytes 11010072
  48.6 2.0 fusion.8
  51.3 404.2 %while.20 = (s32[]{:T(128)}, f32[16,6]{0,1:T(8,128)S(1)}, bf16[16,8192]{1,0:T(8,128)(2,1)S(1)}, bf16[16,28672]{1,0:T(8,128)(2,1)S(1)}, s32[]{:T(128)}, /*index=5...) while((s32[]{:T(128)}, f32[16,6]{0,1:T(8,128)S(1)}, ...), condition=%wide.region_6.7_spmd.clone, body=%wide.region_4.6_spmd.clone.sunk | while | flops 226517776 | bytes 35072120 | solution.py:60
  51.3 0.5 collective-permute-start
  51.7 2.6 collective-permute-start.1
  54.4 16.2 %collective-permute-done.1 = bf16[16,8192]{1,0:T(8,128)(2,1)S(1)} collective-permute-done((bf16[16,8192]{1,0:T(8,128)(2,1)S(1)}, bf16[16,8192]{1,0:T(8,128)(2,1)S(1)}, u32[]{:S(2)}, u32[]{:S(2)}) %collective-permute-start.1) | collective-permute-done | bytes 262176 | tf_op jit(solution)/shard_map/while/body/eval_jaxpr/ppermute | solution.py:12
  70.7 7.3 %fusion.41 = f32[16,192]{1,0:T(8,128)S(1)} fusion(bf16[16,28672]{1,0:T(8,128)(2,1)S(1)} %collective-permute-done, bf16[28672,192]{1,0:T(8,128)(2,1)} %get-tuple-element.378), kind=kOutput, calls=%fused_computation.24.clone.1 | convolution fusion | flops 176160768 | bytes 11939840 | tf_op jit(solution)/shard_map/while/body/eval_jaxpr/dot_general | solution.py:44
  78.0 0.7 convolution_multiply_fusion.3
  78.8 0.2 convolution_add_fusion.2
  79.3 18.2 %collective-permute-done.1 = bf16[16,8192]{1,0:T(8,128)(2,1)S(1)} collective-permute-done((bf16[16,8192]{1,0:T(8,128)(2,1)S(1)}, bf16[16,8192]{1,0:T(8,128)(2,1)S(1)}, u32[]{:S(2)}, u32[]{:S(2)}) %collective-permute-start.1) | collective-permute-done | bytes 262176 | tf_op jit(solution)/shard_map/while/body/eval_jaxpr/ppermute | solution.py:12
  97.5 7.3 %fusion.41 = f32[16,192]{1,0:T(8,128)S(1)} fusion(bf16[16,28672]{1,0:T(8,128)(2,1)S(1)} %collective-permute-done, bf16[28672,192]{1,0:T(8,128)(2,1)} %get-tuple-element.378), kind=kOutput, calls=%fused_computation.24.clone.1 | convolution fusion | flops 176160768 | bytes 11939840 | tf_op jit(solution)/shard_map/while/body/eval_jaxpr/dot_general | solution.py:44
  104.9 0.7 convolution_multiply_fusion.3
  105.7 0.2 convolution_add_fusion.2
  106.2 18.2 %collective-permute-done.1 = bf16[16,8192]{1,0:T(8,128)(2,1)S(1)} collective-permute-done((bf16[16,8192]{1,0:T(8,128)(2,1)S(1)}, bf16[16,8192]{1,0:T(8,128)(2,1)S(1)}, u32[]{:S(2)}, u32[]{:S(2)}) %collective-permute-start.1) | collective-permute-done | bytes 262176 | tf_op jit(solution)/shard_map/while/body/eval_jaxpr/ppermute | solution.py:12
  124.4 7.3 %fusion.41 = f32[16,192]{1,0:T(8,128)S(1)} fusion(bf16[16,28672]{1,0:T(8,128)(2,1)S(1)} %collective-permute-done, bf16[28672,192]{1,0:T(8,128)(2,1)} %get-tuple-element.378), kind=kOutput, calls=%fused_computation.24.clone.1 | convolution fusion | flops 176160768 | bytes 11939840 | tf_op jit(solution)/shard_map/while/body/eval_jaxpr/dot_general | solution.py:44
  131.7 0.7 convolution_multiply_fusion.3
  133.0 18.2 %collective-permute-done.1 = bf16[16,8192]{1,0:T(8,128)(2,1)S(1)} collective-permute-done((bf16[16,8192]{1,0:T(8,128)(2,1)S(1)}, bf16[16,8192]{1,0:T(8,128)(2,1)S(1)}, u32[]{:S(2)}, u32[]{:S(2)}) %collective-permute-start.1) | collective-permute-done | bytes 262176 | tf_op jit(solution)/shard_map/while/body/eval_jaxpr/ppermute | solution.py:12
  151.3 7.3 %fusion.41 = f32[16,192]{1,0:T(8,128)S(1)} fusion(bf16[16,28672]{1,0:T(8,128)(2,1)S(1)} %collective-permute-done, bf16[28672,192]{1,0:T(8,128)(2,1)} %get-tuple-element.378), kind=kOutput, calls=%fused_computation.24.clone.1 | convolution fusion | flops 176160768 | bytes 11939840 | tf_op jit(solution)/shard_map/while/body/eval_jaxpr/dot_general | solution.py:44
  158.6 0.7 convolution_multiply_fusion.3
  159.9 18.2 %collective-permute-done.1 = bf16[16,8192]{1,0:T(8,128)(2,1)S(1)} collective-permute-done((bf16[16,8192]{1,0:T(8,128)(2,1)S(1)}, bf16[16,8192]{1,0:T(8,128)(2,1)S(1)}, u32[]{:S(2)}, u32[]{:S(2)}) %collective-permute-start.1) | collective-permute-done | bytes 262176 | tf_op jit(solution)/shard_map/while/body/eval_jaxpr/ppermute | solution.py:12
  178.2 7.3 %fusion.41 = f32[16,192]{1,0:T(8,128)S(1)} fusion(bf16[16,28672]{1,0:T(8,128)(2,1)S(1)} %collective-permute-done, bf16[28672,192]{1,0:T(8,128)(2,1)} %get-tuple-element.378), kind=kOutput, calls=%fused_computation.24.clone.1 | convolution fusion | flops 176160768 | bytes 11939840 | tf_op jit(solution)/shard_map/while/body/eval_jaxpr/dot_general | solution.py:44
  185.5 0.7 convolution_multiply_fusion.3
  186.8 18.2 %collective-permute-done.1 = bf16[16,8192]{1,0:T(8,128)(2,1)S(1)} collective-permute-done((bf16[16,8192]{1,0:T(8,128)(2,1)S(1)}, bf16[16,8192]{1,0:T(8,128)(2,1)S(1)}, u32[]{:S(2)}, u32[]{:S(2)}) %collective-permute-start.1) | collective-permute-done | bytes 262176 | tf_op jit(solution)/shard_map/while/body/eval_jaxpr/ppermute | solution.py:12
  205.1 7.3 %fusion.41 = f32[16,192]{1,0:T(8,128)S(1)} fusion(bf16[16,28672]{1,0:T(8,128)(2,1)S(1)} %collective-permute-done, bf16[28672,192]{1,0:T(8,128)(2,1)} %get-tuple-element.378), kind=kOutput, calls=%fused_computation.24.clone.1 | convolution fusion | flops 176160768 | bytes 11939840 | tf_op jit(solution)/shard_map/while/body/eval_jaxpr/dot_general | solution.py:44
  212.4 0.7 convolution_multiply_fusion.3
  213.7 18.2 %collective-permute-done.1 = bf16[16,8192]{1,0:T(8,128)(2,1)S(1)} collective-permute-done((bf16[16,8192]{1,0:T(8,128)(2,1)S(1)}, bf16[16,8192]{1,0:T(8,128)(2,1)S(1)}, u32[]{:S(2)}, u32[]{:S(2)}) %collective-permute-start.1) | collective-permute-done | bytes 262176 | tf_op jit(solution)/shard_map/while/body/eval_jaxpr/ppermute | solution.py:12
  231.9 7.3 %fusion.41 = f32[16,192]{1,0:T(8,128)S(1)} fusion(bf16[16,28672]{1,0:T(8,128)(2,1)S(1)} %collective-permute-done, bf16[28672,192]{1,0:T(8,128)(2,1)} %get-tuple-element.378), kind=kOutput, calls=%fused_computation.24.clone.1 | convolution fusion | flops 176160768 | bytes 11939840 | tf_op jit(solution)/shard_map/while/body/eval_jaxpr/dot_general | solution.py:44
  239.3 0.7 convolution_multiply_fusion.3
  240.6 18.2 %collective-permute-done.1 = bf16[16,8192]{1,0:T(8,128)(2,1)S(1)} collective-permute-done((bf16[16,8192]{1,0:T(8,128)(2,1)S(1)}, bf16[16,8192]{1,0:T(8,128)(2,1)S(1)}, u32[]{:S(2)}, u32[]{:S(2)}) %collective-permute-start.1) | collective-permute-done | bytes 262176 | tf_op jit(solution)/shard_map/while/body/eval_jaxpr/ppermute | solution.py:12
  258.8 7.3 %fusion.41 = f32[16,192]{1,0:T(8,128)S(1)} fusion(bf16[16,28672]{1,0:T(8,128)(2,1)S(1)} %collective-permute-done, bf16[28672,192]{1,0:T(8,128)(2,1)} %get-tuple-element.378), kind=kOutput, calls=%fused_computation.24.clone.1 | convolution fusion | flops 176160768 | bytes 11939840 | tf_op jit(solution)/shard_map/while/body/eval_jaxpr/dot_general | solution.py:44
  266.1 0.7 convolution_multiply_fusion.3
  267.5 18.2 %collective-permute-done.1 = bf16[16,8192]{1,0:T(8,128)(2,1)S(1)} collective-permute-done((bf16[16,8192]{1,0:T(8,128)(2,1)S(1)}, bf16[16,8192]{1,0:T(8,128)(2,1)S(1)}, u32[]{:S(2)}, u32[]{:S(2)}) %collective-permute-start.1) | collective-permute-done | bytes 262176 | tf_op jit(solution)/shard_map/while/body/eval_jaxpr/ppermute | solution.py:12
  285.7 7.3 %fusion.41 = f32[16,192]{1,0:T(8,128)S(1)} fusion(bf16[16,28672]{1,0:T(8,128)(2,1)S(1)} %collective-permute-done, bf16[28672,192]{1,0:T(8,128)(2,1)} %get-tuple-element.378), kind=kOutput, calls=%fused_computation.24.clone.1 | convolution fusion | flops 176160768 | bytes 11939840 | tf_op jit(solution)/shard_map/while/body/eval_jaxpr/dot_general | solution.py:44
  293.0 0.7 convolution_multiply_fusion.3
  294.3 18.2 %collective-permute-done.1 = bf16[16,8192]{1,0:T(8,128)(2,1)S(1)} collective-permute-done((bf16[16,8192]{1,0:T(8,128)(2,1)S(1)}, bf16[16,8192]{1,0:T(8,128)(2,1)S(1)}, u32[]{:S(2)}, u32[]{:S(2)}) %collective-permute-start.1) | collective-permute-done | bytes 262176 | tf_op jit(solution)/shard_map/while/body/eval_jaxpr/ppermute | solution.py:12
  312.6 7.3 %fusion.41 = f32[16,192]{1,0:T(8,128)S(1)} fusion(bf16[16,28672]{1,0:T(8,128)(2,1)S(1)} %collective-permute-done, bf16[28672,192]{1,0:T(8,128)(2,1)} %get-tuple-element.378), kind=kOutput, calls=%fused_computation.24.clone.1 | convolution fusion | flops 176160768 | bytes 11939840 | tf_op jit(solution)/shard_map/while/body/eval_jaxpr/dot_general | solution.py:44
  319.9 0.7 convolution_multiply_fusion.3
  321.2 18.2 %collective-permute-done.1 = bf16[16,8192]{1,0:T(8,128)(2,1)S(1)} collective-permute-done((bf16[16,8192]{1,0:T(8,128)(2,1)S(1)}, bf16[16,8192]{1,0:T(8,128)(2,1)S(1)}, u32[]{:S(2)}, u32[]{:S(2)}) %collective-permute-start.1) | collective-permute-done | bytes 262176 | tf_op jit(solution)/shard_map/while/body/eval_jaxpr/ppermute | solution.py:12
  339.5 7.3 %fusion.41 = f32[16,192]{1,0:T(8,128)S(1)} fusion(bf16[16,28672]{1,0:T(8,128)(2,1)S(1)} %collective-permute-done, bf16[28672,192]{1,0:T(8,128)(2,1)} %get-tuple-element.378), kind=kOutput, calls=%fused_computation.24.clone.1 | convolution fusion | flops 176160768 | bytes 11939840 | tf_op jit(solution)/shard_map/while/body/eval_jaxpr/dot_general | solution.py:44
  346.8 0.7 convolution_multiply_fusion.3
  348.1 18.2 %collective-permute-done.1 = bf16[16,8192]{1,0:T(8,128)(2,1)S(1)} collective-permute-done((bf16[16,8192]{1,0:T(8,128)(2,1)S(1)}, bf16[16,8192]{1,0:T(8,128)(2,1)S(1)}, u32[]{:S(2)}, u32[]{:S(2)}) %collective-permute-start.1) | collective-permute-done | bytes 262176 | tf_op jit(solution)/shard_map/while/body/eval_jaxpr/ppermute | solution.py:12
  366.4 7.3 %fusion.41 = f32[16,192]{1,0:T(8,128)S(1)} fusion(bf16[16,28672]{1,0:T(8,128)(2,1)S(1)} %collective-permute-done, bf16[28672,192]{1,0:T(8,128)(2,1)} %get-tuple-element.378), kind=kOutput, calls=%fused_computation.24.clone.1 | convolution fusion | flops 176160768 | bytes 11939840 | tf_op jit(solution)/shard_map/while/body/eval_jaxpr/dot_general | solution.py:44
  373.7 0.7 convolution_multiply_fusion.3
  375.0 18.2 %collective-permute-done.1 = bf16[16,8192]{1,0:T(8,128)(2,1)S(1)} collective-permute-done((bf16[16,8192]{1,0:T(8,128)(2,1)S(1)}, bf16[16,8192]{1,0:T(8,128)(2,1)S(1)}, u32[]{:S(2)}, u32[]{:S(2)}) %collective-permute-start.1) | collective-permute-done | bytes 262176 | tf_op jit(solution)/shard_map/while/body/eval_jaxpr/ppermute | solution.py:12
  393.2 7.3 %fusion.41 = f32[16,192]{1,0:T(8,128)S(1)} fusion(bf16[16,28672]{1,0:T(8,128)(2,1)S(1)} %collective-permute-done, bf16[28672,192]{1,0:T(8,128)(2,1)} %get-tuple-element.378), kind=kOutput, calls=%fused_computation.24.clone.1 | convolution fusion | flops 176160768 | bytes 11939840 | tf_op jit(solution)/shard_map/while/body/eval_jaxpr/dot_general | solution.py:44
  400.6 0.7 convolution_multiply_fusion.3
  401.9 18.2 %collective-permute-done.1 = bf16[16,8192]{1,0:T(8,128)(2,1)S(1)} collective-permute-done((bf16[16,8192]{1,0:T(8,128)(2,1)S(1)}, bf16[16,8192]{1,0:T(8,128)(2,1)S(1)}, u32[]{:S(2)}, u32[]{:S(2)}) %collective-permute-start.1) | collective-permute-done | bytes 262176 | tf_op jit(solution)/shard_map/while/body/eval_jaxpr/ppermute | solution.py:12
  420.1 7.3 %fusion.41 = f32[16,192]{1,0:T(8,128)S(1)} fusion(bf16[16,28672]{1,0:T(8,128)(2,1)S(1)} %collective-permute-done, bf16[28672,192]{1,0:T(8,128)(2,1)} %get-tuple-element.378), kind=kOutput, calls=%fused_computation.24.clone.1 | convolution fusion | flops 176160768 | bytes 11939840 | tf_op jit(solution)/shard_map/while/body/eval_jaxpr/dot_general | solution.py:44
  427.4 0.7 convolution_multiply_fusion.3
  428.7 18.2 %collective-permute-done.1 = bf16[16,8192]{1,0:T(8,128)(2,1)S(1)} collective-permute-done((bf16[16,8192]{1,0:T(8,128)(2,1)S(1)}, bf16[16,8192]{1,0:T(8,128)(2,1)S(1)}, u32[]{:S(2)}, u32[]{:S(2)}) %collective-permute-start.1) | collective-permute-done | bytes 262176 | tf_op jit(solution)/shard_map/while/body/eval_jaxpr/ppermute | solution.py:12
  447.0 7.3 %fusion.41 = f32[16,192]{1,0:T(8,128)S(1)} fusion(bf16[16,28672]{1,0:T(8,128)(2,1)S(1)} %collective-permute-done, bf16[28672,192]{1,0:T(8,128)(2,1)} %get-tuple-element.378), kind=kOutput, calls=%fused_computation.24.clone.1 | convolution fusion | flops 176160768 | bytes 11939840 | tf_op jit(solution)/shard_map/while/body/eval_jaxpr/dot_general | solution.py:44
  454.3 0.7 convolution_multiply_fusion.3
  455.5 0.6 copy-done.5
  (177 shorter events, 9.0 us)
Async XLA Ops:
  13.7 2.0 copy-start.1
  16.3 16.8 %copy-start.3 = (f32[28672]{0:T(1024)S(1)}, f32[28672]{0:T(1024)}, u32[]{:S(2)}) copy-start(f32[28672]{0:T(1024)} %param.14) | copy-start | bytes 344068
  43.4 5.2 %copy-start = (bf16[28672,192]{1,0:T(8,128)(2,1)}, bf16[28672,192]{1,0:T(8,128)(2,1)S(1)}, u32[]{:S(2)}) copy-start(bf16[28672,192]{1,0:T(8,128)(2,1)S(1)} %divide_convert_fusion) | copy-start | bytes 33030148
  48.6 2.2 copy-start.4
  51.3 19.4 %collective-permute-start = (bf16[16,28672]{1,0:T(8,128)(2,1)S(1)}, bf16[16,28672]{1,0:T(8,128)(2,1)S(1)}, u32[]{:S(2)}, u32[]{:S(2)}) collective-permute-start(bf16[16,28672]{1,0:T(8,128)(2,1)S(1)} %get-tuple-element.359), channel_id=1, source_target_pairs={{0,1},{1,2},{2,3},{3,4},{4,5},{5,6},{6,7},{7,8},{8,9},{9,10},{10,1... | collective-permute-start | bytes 2752520 | tf_op jit(solution)/shard_map/while/body/eval_jaxpr/ppermute | solution.py:12
  51.7 18.9 %collective-permute-start.1 = (bf16[16,8192]{1,0:T(8,128)(2,1)S(1)}, bf16[16,8192]{1,0:T(8,128)(2,1)S(1)}, u32[]{:S(2)}, u32[]{:S(2)}) collective-permute-start(bf16[16,8192]{1,0:T(8,128)(2,1)S(1)} %get-tuple-element.358), channel_id=1, source_target_pairs={{0,1},{1,2},{2,3},{3,4},{4,5},{5,6},{6,7},{7,8},{8,9},{9,10},{10,1... | collective-permute-start | bytes 786440 | tf_op jit(solution)/shard_map/while/body/eval_jaxpr/ppermute | solution.py:12
  70.7 7.3 %copy-start.2 = (bf16[8192,192]{1,0:T(8,128)(2,1)S(1)}, bf16[8192,192]{1,0:T(8,128)(2,1)}, u32[]{:S(2)}) copy-start(bf16[8192,192]{1,0:T(8,128)(2,1)} %get-tuple-element.377) | copy-start | bytes 9437188 | tf_op jit(solution)/shard_map/while
  79.1 18.4 %collective-permute-start = (bf16[16,28672]{1,0:T(8,128)(2,1)S(1)}, bf16[16,28672]{1,0:T(8,128)(2,1)S(1)}, u32[]{:S(2)}, u32[]{:S(2)}) collective-permute-start(bf16[16,28672]{1,0:T(8,128)(2,1)S(1)} %get-tuple-element.359), channel_id=1, source_target_pairs={{0,1},{1,2},{2,3},{3,4},{4,5},{5,6},{6,7},{7,8},{8,9},{9,10},{10,1... | collective-permute-start | bytes 2752520 | tf_op jit(solution)/shard_map/while/body/eval_jaxpr/ppermute | solution.py:12
  79.2 18.3 %collective-permute-start.1 = (bf16[16,8192]{1,0:T(8,128)(2,1)S(1)}, bf16[16,8192]{1,0:T(8,128)(2,1)S(1)}, u32[]{:S(2)}, u32[]{:S(2)}) collective-permute-start(bf16[16,8192]{1,0:T(8,128)(2,1)S(1)} %get-tuple-element.358), channel_id=1, source_target_pairs={{0,1},{1,2},{2,3},{3,4},{4,5},{5,6},{6,7},{7,8},{8,9},{9,10},{10,1... | collective-permute-start | bytes 786440 | tf_op jit(solution)/shard_map/while/body/eval_jaxpr/ppermute | solution.py:12
  97.5 7.3 %copy-start.2 = (bf16[8192,192]{1,0:T(8,128)(2,1)S(1)}, bf16[8192,192]{1,0:T(8,128)(2,1)}, u32[]{:S(2)}) copy-start(bf16[8192,192]{1,0:T(8,128)(2,1)} %get-tuple-element.377) | copy-start | bytes 9437188 | tf_op jit(solution)/shard_map/while
  106.0 18.4 %collective-permute-start = (bf16[16,28672]{1,0:T(8,128)(2,1)S(1)}, bf16[16,28672]{1,0:T(8,128)(2,1)S(1)}, u32[]{:S(2)}, u32[]{:S(2)}) collective-permute-start(bf16[16,28672]{1,0:T(8,128)(2,1)S(1)} %get-tuple-element.359), channel_id=1, source_target_pairs={{0,1},{1,2},{2,3},{3,4},{4,5},{5,6},{6,7},{7,8},{8,9},{9,10},{10,1... | collective-permute-start | bytes 2752520 | tf_op jit(solution)/shard_map/while/body/eval_jaxpr/ppermute | solution.py:12
  106.1 18.3 %collective-permute-start.1 = (bf16[16,8192]{1,0:T(8,128)(2,1)S(1)}, bf16[16,8192]{1,0:T(8,128)(2,1)S(1)}, u32[]{:S(2)}, u32[]{:S(2)}) collective-permute-start(bf16[16,8192]{1,0:T(8,128)(2,1)S(1)} %get-tuple-element.358), channel_id=1, source_target_pairs={{0,1},{1,2},{2,3},{3,4},{4,5},{5,6},{6,7},{7,8},{8,9},{9,10},{10,1... | collective-permute-start | bytes 786440 | tf_op jit(solution)/shard_map/while/body/eval_jaxpr/ppermute | solution.py:12
  124.4 7.3 %copy-start.2 = (bf16[8192,192]{1,0:T(8,128)(2,1)S(1)}, bf16[8192,192]{1,0:T(8,128)(2,1)}, u32[]{:S(2)}) copy-start(bf16[8192,192]{1,0:T(8,128)(2,1)} %get-tuple-element.377) | copy-start | bytes 9437188 | tf_op jit(solution)/shard_map/while
  132.9 18.4 %collective-permute-start = (bf16[16,28672]{1,0:T(8,128)(2,1)S(1)}, bf16[16,28672]{1,0:T(8,128)(2,1)S(1)}, u32[]{:S(2)}, u32[]{:S(2)}) collective-permute-start(bf16[16,28672]{1,0:T(8,128)(2,1)S(1)} %get-tuple-element.359), channel_id=1, source_target_pairs={{0,1},{1,2},{2,3},{3,4},{4,5},{5,6},{6,7},{7,8},{8,9},{9,10},{10,1... | collective-permute-start | bytes 2752520 | tf_op jit(solution)/shard_map/while/body/eval_jaxpr/ppermute | solution.py:12
  132.9 18.3 %collective-permute-start.1 = (bf16[16,8192]{1,0:T(8,128)(2,1)S(1)}, bf16[16,8192]{1,0:T(8,128)(2,1)S(1)}, u32[]{:S(2)}, u32[]{:S(2)}) collective-permute-start(bf16[16,8192]{1,0:T(8,128)(2,1)S(1)} %get-tuple-element.358), channel_id=1, source_target_pairs={{0,1},{1,2},{2,3},{3,4},{4,5},{5,6},{6,7},{7,8},{8,9},{9,10},{10,1... | collective-permute-start | bytes 786440 | tf_op jit(solution)/shard_map/while/body/eval_jaxpr/ppermute | solution.py:12
  151.3 7.3 %copy-start.2 = (bf16[8192,192]{1,0:T(8,128)(2,1)S(1)}, bf16[8192,192]{1,0:T(8,128)(2,1)}, u32[]{:S(2)}) copy-start(bf16[8192,192]{1,0:T(8,128)(2,1)} %get-tuple-element.377) | copy-start | bytes 9437188 | tf_op jit(solution)/shard_map/while
  159.8 18.4 %collective-permute-start = (bf16[16,28672]{1,0:T(8,128)(2,1)S(1)}, bf16[16,28672]{1,0:T(8,128)(2,1)S(1)}, u32[]{:S(2)}, u32[]{:S(2)}) collective-permute-start(bf16[16,28672]{1,0:T(8,128)(2,1)S(1)} %get-tuple-element.359), channel_id=1, source_target_pairs={{0,1},{1,2},{2,3},{3,4},{4,5},{5,6},{6,7},{7,8},{8,9},{9,10},{10,1... | collective-permute-start | bytes 2752520 | tf_op jit(solution)/shard_map/while/body/eval_jaxpr/ppermute | solution.py:12
  159.8 18.3 %collective-permute-start.1 = (bf16[16,8192]{1,0:T(8,128)(2,1)S(1)}, bf16[16,8192]{1,0:T(8,128)(2,1)S(1)}, u32[]{:S(2)}, u32[]{:S(2)}) collective-permute-start(bf16[16,8192]{1,0:T(8,128)(2,1)S(1)} %get-tuple-element.358), channel_id=1, source_target_pairs={{0,1},{1,2},{2,3},{3,4},{4,5},{5,6},{6,7},{7,8},{8,9},{9,10},{10,1... | collective-permute-start | bytes 786440 | tf_op jit(solution)/shard_map/while/body/eval_jaxpr/ppermute | solution.py:12
  178.2 7.3 %copy-start.2 = (bf16[8192,192]{1,0:T(8,128)(2,1)S(1)}, bf16[8192,192]{1,0:T(8,128)(2,1)}, u32[]{:S(2)}) copy-start(bf16[8192,192]{1,0:T(8,128)(2,1)} %get-tuple-element.377) | copy-start | bytes 9437188 | tf_op jit(solution)/shard_map/while
  186.6 18.4 %collective-permute-start = (bf16[16,28672]{1,0:T(8,128)(2,1)S(1)}, bf16[16,28672]{1,0:T(8,128)(2,1)S(1)}, u32[]{:S(2)}, u32[]{:S(2)}) collective-permute-start(bf16[16,28672]{1,0:T(8,128)(2,1)S(1)} %get-tuple-element.359), channel_id=1, source_target_pairs={{0,1},{1,2},{2,3},{3,4},{4,5},{5,6},{6,7},{7,8},{8,9},{9,10},{10,1... | collective-permute-start | bytes 2752520 | tf_op jit(solution)/shard_map/while/body/eval_jaxpr/ppermute | solution.py:12
  186.7 18.3 %collective-permute-start.1 = (bf16[16,8192]{1,0:T(8,128)(2,1)S(1)}, bf16[16,8192]{1,0:T(8,128)(2,1)S(1)}, u32[]{:S(2)}, u32[]{:S(2)}) collective-permute-start(bf16[16,8192]{1,0:T(8,128)(2,1)S(1)} %get-tuple-element.358), channel_id=1, source_target_pairs={{0,1},{1,2},{2,3},{3,4},{4,5},{5,6},{6,7},{7,8},{8,9},{9,10},{10,1... | collective-permute-start | bytes 786440 | tf_op jit(solution)/shard_map/while/body/eval_jaxpr/ppermute | solution.py:12
  205.1 7.3 %copy-start.2 = (bf16[8192,192]{1,0:T(8,128)(2,1)S(1)}, bf16[8192,192]{1,0:T(8,128)(2,1)}, u32[]{:S(2)}) copy-start(bf16[8192,192]{1,0:T(8,128)(2,1)} %get-tuple-element.377) | copy-start | bytes 9437188 | tf_op jit(solution)/shard_map/while
  213.5 18.4 %collective-permute-start = (bf16[16,28672]{1,0:T(8,128)(2,1)S(1)}, bf16[16,28672]{1,0:T(8,128)(2,1)S(1)}, u32[]{:S(2)}, u32[]{:S(2)}) collective-permute-start(bf16[16,28672]{1,0:T(8,128)(2,1)S(1)} %get-tuple-element.359), channel_id=1, source_target_pairs={{0,1},{1,2},{2,3},{3,4},{4,5},{5,6},{6,7},{7,8},{8,9},{9,10},{10,1... | collective-permute-start | bytes 2752520 | tf_op jit(solution)/shard_map/while/body/eval_jaxpr/ppermute | solution.py:12
  213.6 18.3 %collective-permute-start.1 = (bf16[16,8192]{1,0:T(8,128)(2,1)S(1)}, bf16[16,8192]{1,0:T(8,128)(2,1)S(1)}, u32[]{:S(2)}, u32[]{:S(2)}) collective-permute-start(bf16[16,8192]{1,0:T(8,128)(2,1)S(1)} %get-tuple-element.358), channel_id=1, source_target_pairs={{0,1},{1,2},{2,3},{3,4},{4,5},{5,6},{6,7},{7,8},{8,9},{9,10},{10,1... | collective-permute-start | bytes 786440 | tf_op jit(solution)/shard_map/while/body/eval_jaxpr/ppermute | solution.py:12
  231.9 7.3 %copy-start.2 = (bf16[8192,192]{1,0:T(8,128)(2,1)S(1)}, bf16[8192,192]{1,0:T(8,128)(2,1)}, u32[]{:S(2)}) copy-start(bf16[8192,192]{1,0:T(8,128)(2,1)} %get-tuple-element.377) | copy-start | bytes 9437188 | tf_op jit(solution)/shard_map/while
  240.4 18.4 %collective-permute-start = (bf16[16,28672]{1,0:T(8,128)(2,1)S(1)}, bf16[16,28672]{1,0:T(8,128)(2,1)S(1)}, u32[]{:S(2)}, u32[]{:S(2)}) collective-permute-start(bf16[16,28672]{1,0:T(8,128)(2,1)S(1)} %get-tuple-element.359), channel_id=1, source_target_pairs={{0,1},{1,2},{2,3},{3,4},{4,5},{5,6},{6,7},{7,8},{8,9},{9,10},{10,1... | collective-permute-start | bytes 2752520 | tf_op jit(solution)/shard_map/while/body/eval_jaxpr/ppermute | solution.py:12
  240.5 18.3 %collective-permute-start.1 = (bf16[16,8192]{1,0:T(8,128)(2,1)S(1)}, bf16[16,8192]{1,0:T(8,128)(2,1)S(1)}, u32[]{:S(2)}, u32[]{:S(2)}) collective-permute-start(bf16[16,8192]{1,0:T(8,128)(2,1)S(1)} %get-tuple-element.358), channel_id=1, source_target_pairs={{0,1},{1,2},{2,3},{3,4},{4,5},{5,6},{6,7},{7,8},{8,9},{9,10},{10,1... | collective-permute-start | bytes 786440 | tf_op jit(solution)/shard_map/while/body/eval_jaxpr/ppermute | solution.py:12
  258.8 7.3 %copy-start.2 = (bf16[8192,192]{1,0:T(8,128)(2,1)S(1)}, bf16[8192,192]{1,0:T(8,128)(2,1)}, u32[]{:S(2)}) copy-start(bf16[8192,192]{1,0:T(8,128)(2,1)} %get-tuple-element.377) | copy-start | bytes 9437188 | tf_op jit(solution)/shard_map/while
  267.3 18.4 %collective-permute-start = (bf16[16,28672]{1,0:T(8,128)(2,1)S(1)}, bf16[16,28672]{1,0:T(8,128)(2,1)S(1)}, u32[]{:S(2)}, u32[]{:S(2)}) collective-permute-start(bf16[16,28672]{1,0:T(8,128)(2,1)S(1)} %get-tuple-element.359), channel_id=1, source_target_pairs={{0,1},{1,2},{2,3},{3,4},{4,5},{5,6},{6,7},{7,8},{8,9},{9,10},{10,1... | collective-permute-start | bytes 2752520 | tf_op jit(solution)/shard_map/while/body/eval_jaxpr/ppermute | solution.py:12
  267.4 18.3 %collective-permute-start.1 = (bf16[16,8192]{1,0:T(8,128)(2,1)S(1)}, bf16[16,8192]{1,0:T(8,128)(2,1)S(1)}, u32[]{:S(2)}, u32[]{:S(2)}) collective-permute-start(bf16[16,8192]{1,0:T(8,128)(2,1)S(1)} %get-tuple-element.358), channel_id=1, source_target_pairs={{0,1},{1,2},{2,3},{3,4},{4,5},{5,6},{6,7},{7,8},{8,9},{9,10},{10,1... | collective-permute-start | bytes 786440 | tf_op jit(solution)/shard_map/while/body/eval_jaxpr/ppermute | solution.py:12
  285.7 7.3 %copy-start.2 = (bf16[8192,192]{1,0:T(8,128)(2,1)S(1)}, bf16[8192,192]{1,0:T(8,128)(2,1)}, u32[]{:S(2)}) copy-start(bf16[8192,192]{1,0:T(8,128)(2,1)} %get-tuple-element.377) | copy-start | bytes 9437188 | tf_op jit(solution)/shard_map/while
  294.2 18.4 %collective-permute-start = (bf16[16,28672]{1,0:T(8,128)(2,1)S(1)}, bf16[16,28672]{1,0:T(8,128)(2,1)S(1)}, u32[]{:S(2)}, u32[]{:S(2)}) collective-permute-start(bf16[16,28672]{1,0:T(8,128)(2,1)S(1)} %get-tuple-element.359), channel_id=1, source_target_pairs={{0,1},{1,2},{2,3},{3,4},{4,5},{5,6},{6,7},{7,8},{8,9},{9,10},{10,1... | collective-permute-start | bytes 2752520 | tf_op jit(solution)/shard_map/while/body/eval_jaxpr/ppermute | solution.py:12
  294.2 18.3 %collective-permute-start.1 = (bf16[16,8192]{1,0:T(8,128)(2,1)S(1)}, bf16[16,8192]{1,0:T(8,128)(2,1)S(1)}, u32[]{:S(2)}, u32[]{:S(2)}) collective-permute-start(bf16[16,8192]{1,0:T(8,128)(2,1)S(1)} %get-tuple-element.358), channel_id=1, source_target_pairs={{0,1},{1,2},{2,3},{3,4},{4,5},{5,6},{6,7},{7,8},{8,9},{9,10},{10,1... | collective-permute-start | bytes 786440 | tf_op jit(solution)/shard_map/while/body/eval_jaxpr/ppermute | solution.py:12
  312.6 7.3 %copy-start.2 = (bf16[8192,192]{1,0:T(8,128)(2,1)S(1)}, bf16[8192,192]{1,0:T(8,128)(2,1)}, u32[]{:S(2)}) copy-start(bf16[8192,192]{1,0:T(8,128)(2,1)} %get-tuple-element.377) | copy-start | bytes 9437188 | tf_op jit(solution)/shard_map/while
  321.1 18.4 %collective-permute-start = (bf16[16,28672]{1,0:T(8,128)(2,1)S(1)}, bf16[16,28672]{1,0:T(8,128)(2,1)S(1)}, u32[]{:S(2)}, u32[]{:S(2)}) collective-permute-start(bf16[16,28672]{1,0:T(8,128)(2,1)S(1)} %get-tuple-element.359), channel_id=1, source_target_pairs={{0,1},{1,2},{2,3},{3,4},{4,5},{5,6},{6,7},{7,8},{8,9},{9,10},{10,1... | collective-permute-start | bytes 2752520 | tf_op jit(solution)/shard_map/while/body/eval_jaxpr/ppermute | solution.py:12
  321.1 18.3 %collective-permute-start.1 = (bf16[16,8192]{1,0:T(8,128)(2,1)S(1)}, bf16[16,8192]{1,0:T(8,128)(2,1)S(1)}, u32[]{:S(2)}, u32[]{:S(2)}) collective-permute-start(bf16[16,8192]{1,0:T(8,128)(2,1)S(1)} %get-tuple-element.358), channel_id=1, source_target_pairs={{0,1},{1,2},{2,3},{3,4},{4,5},{5,6},{6,7},{7,8},{8,9},{9,10},{10,1... | collective-permute-start | bytes 786440 | tf_op jit(solution)/shard_map/while/body/eval_jaxpr/ppermute | solution.py:12
  339.5 7.3 %copy-start.2 = (bf16[8192,192]{1,0:T(8,128)(2,1)S(1)}, bf16[8192,192]{1,0:T(8,128)(2,1)}, u32[]{:S(2)}) copy-start(bf16[8192,192]{1,0:T(8,128)(2,1)} %get-tuple-element.377) | copy-start | bytes 9437188 | tf_op jit(solution)/shard_map/while
  347.9 18.4 %collective-permute-start = (bf16[16,28672]{1,0:T(8,128)(2,1)S(1)}, bf16[16,28672]{1,0:T(8,128)(2,1)S(1)}, u32[]{:S(2)}, u32[]{:S(2)}) collective-permute-start(bf16[16,28672]{1,0:T(8,128)(2,1)S(1)} %get-tuple-element.359), channel_id=1, source_target_pairs={{0,1},{1,2},{2,3},{3,4},{4,5},{5,6},{6,7},{7,8},{8,9},{9,10},{10,1... | collective-permute-start | bytes 2752520 | tf_op jit(solution)/shard_map/while/body/eval_jaxpr/ppermute | solution.py:12
  348.0 18.3 %collective-permute-start.1 = (bf16[16,8192]{1,0:T(8,128)(2,1)S(1)}, bf16[16,8192]{1,0:T(8,128)(2,1)S(1)}, u32[]{:S(2)}, u32[]{:S(2)}) collective-permute-start(bf16[16,8192]{1,0:T(8,128)(2,1)S(1)} %get-tuple-element.358), channel_id=1, source_target_pairs={{0,1},{1,2},{2,3},{3,4},{4,5},{5,6},{6,7},{7,8},{8,9},{9,10},{10,1... | collective-permute-start | bytes 786440 | tf_op jit(solution)/shard_map/while/body/eval_jaxpr/ppermute | solution.py:12
  366.3 7.3 %copy-start.2 = (bf16[8192,192]{1,0:T(8,128)(2,1)S(1)}, bf16[8192,192]{1,0:T(8,128)(2,1)}, u32[]{:S(2)}) copy-start(bf16[8192,192]{1,0:T(8,128)(2,1)} %get-tuple-element.377) | copy-start | bytes 9437188 | tf_op jit(solution)/shard_map/while
  374.8 18.4 %collective-permute-start = (bf16[16,28672]{1,0:T(8,128)(2,1)S(1)}, bf16[16,28672]{1,0:T(8,128)(2,1)S(1)}, u32[]{:S(2)}, u32[]{:S(2)}) collective-permute-start(bf16[16,28672]{1,0:T(8,128)(2,1)S(1)} %get-tuple-element.359), channel_id=1, source_target_pairs={{0,1},{1,2},{2,3},{3,4},{4,5},{5,6},{6,7},{7,8},{8,9},{9,10},{10,1... | collective-permute-start | bytes 2752520 | tf_op jit(solution)/shard_map/while/body/eval_jaxpr/ppermute | solution.py:12
  374.9 18.3 %collective-permute-start.1 = (bf16[16,8192]{1,0:T(8,128)(2,1)S(1)}, bf16[16,8192]{1,0:T(8,128)(2,1)S(1)}, u32[]{:S(2)}, u32[]{:S(2)}) collective-permute-start(bf16[16,8192]{1,0:T(8,128)(2,1)S(1)} %get-tuple-element.358), channel_id=1, source_target_pairs={{0,1},{1,2},{2,3},{3,4},{4,5},{5,6},{6,7},{7,8},{8,9},{9,10},{10,1... | collective-permute-start | bytes 786440 | tf_op jit(solution)/shard_map/while/body/eval_jaxpr/ppermute | solution.py:12
  393.2 7.3 %copy-start.2 = (bf16[8192,192]{1,0:T(8,128)(2,1)S(1)}, bf16[8192,192]{1,0:T(8,128)(2,1)}, u32[]{:S(2)}) copy-start(bf16[8192,192]{1,0:T(8,128)(2,1)} %get-tuple-element.377) | copy-start | bytes 9437188 | tf_op jit(solution)/shard_map/while
  401.7 18.4 %collective-permute-start = (bf16[16,28672]{1,0:T(8,128)(2,1)S(1)}, bf16[16,28672]{1,0:T(8,128)(2,1)S(1)}, u32[]{:S(2)}, u32[]{:S(2)}) collective-permute-start(bf16[16,28672]{1,0:T(8,128)(2,1)S(1)} %get-tuple-element.359), channel_id=1, source_target_pairs={{0,1},{1,2},{2,3},{3,4},{4,5},{5,6},{6,7},{7,8},{8,9},{9,10},{10,1... | collective-permute-start | bytes 2752520 | tf_op jit(solution)/shard_map/while/body/eval_jaxpr/ppermute | solution.py:12
  401.8 18.3 %collective-permute-start.1 = (bf16[16,8192]{1,0:T(8,128)(2,1)S(1)}, bf16[16,8192]{1,0:T(8,128)(2,1)S(1)}, u32[]{:S(2)}, u32[]{:S(2)}) collective-permute-start(bf16[16,8192]{1,0:T(8,128)(2,1)S(1)} %get-tuple-element.358), channel_id=1, source_target_pairs={{0,1},{1,2},{2,3},{3,4},{4,5},{5,6},{6,7},{7,8},{8,9},{9,10},{10,1... | collective-permute-start | bytes 786440 | tf_op jit(solution)/shard_map/while/body/eval_jaxpr/ppermute | solution.py:12
  420.1 7.3 %copy-start.2 = (bf16[8192,192]{1,0:T(8,128)(2,1)S(1)}, bf16[8192,192]{1,0:T(8,128)(2,1)}, u32[]{:S(2)}) copy-start(bf16[8192,192]{1,0:T(8,128)(2,1)} %get-tuple-element.377) | copy-start | bytes 9437188 | tf_op jit(solution)/shard_map/while
  428.6 18.4 %collective-permute-start = (bf16[16,28672]{1,0:T(8,128)(2,1)S(1)}, bf16[16,28672]{1,0:T(8,128)(2,1)S(1)}, u32[]{:S(2)}, u32[]{:S(2)}) collective-permute-start(bf16[16,28672]{1,0:T(8,128)(2,1)S(1)} %get-tuple-element.359), channel_id=1, source_target_pairs={{0,1},{1,2},{2,3},{3,4},{4,5},{5,6},{6,7},{7,8},{8,9},{9,10},{10,1... | collective-permute-start | bytes 2752520 | tf_op jit(solution)/shard_map/while/body/eval_jaxpr/ppermute | solution.py:12
  428.6 18.3 %collective-permute-start.1 = (bf16[16,8192]{1,0:T(8,128)(2,1)S(1)}, bf16[16,8192]{1,0:T(8,128)(2,1)S(1)}, u32[]{:S(2)}, u32[]{:S(2)}) collective-permute-start(bf16[16,8192]{1,0:T(8,128)(2,1)S(1)} %get-tuple-element.358), channel_id=1, source_target_pairs={{0,1},{1,2},{2,3},{3,4},{4,5},{5,6},{6,7},{7,8},{8,9},{9,10},{10,1... | collective-permute-start | bytes 786440 | tf_op jit(solution)/shard_map/while/body/eval_jaxpr/ppermute | solution.py:12
  447.0 7.3 %copy-start.2 = (bf16[8192,192]{1,0:T(8,128)(2,1)S(1)}, bf16[8192,192]{1,0:T(8,128)(2,1)}, u32[]{:S(2)}) copy-start(bf16[8192,192]{1,0:T(8,128)(2,1)} %get-tuple-element.377) | copy-start | bytes 9437188 | tf_op jit(solution)/shard_map/while
  455.5 0.6 copy-start.5
where the time goes:
time: 457 us; the launch traced here: 456 us
  waiting for transfers between devices  271 us (59%)
  matrix products  125 us (27%)
  local copies, waits for them, and re-layouts  35.4 us (8%)
  other arithmetic  16.4 us (4%)
  starting transfers between devices  4.73 us (1%)
    ppermute x30, waiting for transfers between devices, from_behind(): return lax.ppermute(value, axis, pairs)  271 us
    dot_general x16, matrix products, accumulate(): grad_proj = jnp.dot(grad_rows, grad_pre, preferred_element_type=jnp.float32)  112 us
    unnamed x14, local copies, waits for them, and re-layouts  32.6 us
    convert_element_type x2, other arithmetic, precondition(): (factors.astype(jnp.float32) / (eigen + damping)[:, None]).astype(jnp.bfl...  11.8 us
    dot_general x16, matrix products, accumulate(): act_proj = jnp.dot(act_rows, act_pre, preferred_element_type=jnp.float32)  10.6 us
  transfers between devices with their start and end apart: 30, of which 15 were waited for; matrix products, arithmetic and copies ran while one was open for 0% of the time, Pallas kernels for 0%

commit v1 on v0

v1 whole, which is shorter than its diff:
```python
import functools

import jax
import jax.numpy as jnp
from jax import lax
from jax.experimental import pallas as pl
from jax.experimental.pallas import tpu as pltpu
from jax.sharding import PartitionSpec as P

RANK = 32
CHUNK = 2048
LAG = 1
SWAP_FIRST = (6, 3)
RAW = 3
MESH = pl.DeviceIdType.MESH


def kernel(
    lines, tok_act, tok_grad, fac_act, fac_grad, eig_act, eig_grad, lengths, out,
    gat, raw, pre, recip, acc, load_sem, raw_sem, recv_sem, send_sem,
):
    chunks, tokens, width = gat.shape
    rows = tok_act.shape[0]
    count = tokens // rows
    depth = count // (2 * lines)
    act_chunks = tok_act.shape[1] // width
    me = lax.axis_index("blk")
    core = me % 2
    line = (me // 2) % lines
    place = me // (2 * lines)

    def block(at, ln, co):
        return (at * lines + ln) * 2 + co

    ahead, behind = block(place + 1, line, core), block(place - 1, line, core)
    across, sibling = block(place, lines - 1 - line, core), block(place, line, 1 - core)
    has_ahead, has_behind = place < depth - 1, place > 0

    def piece(c, owner):
        return gat.at[c, pl.ds(pl.multiple_of(owner * rows, rows), rows), :]

    def copy(link, c, owner, target):
        ref = piece(c, owner)
        return pltpu.make_async_remote_copy(
            src_ref=ref, dst_ref=ref,
            send_sem=send_sem.at[link, c, owner // 2], recv_sem=recv_sem.at[c, owner],
            device_id={"blk": target}, device_id_type=MESH,
        )

    def arrived(c, owner):
        copy(0, c, owner, sibling).wait_recv()

    for c in range(chunks):
        if c < act_chunks:
            source = tok_act.at[:, pl.ds(c * width, width)]
        else:
            source = tok_grad.at[:, pl.ds((c - act_chunks) * width, width)]
        pltpu.make_async_copy(source, piece(c, me), load_sem.at[c]).start()

    def fetch(p):
        slot = raw.at[lax.rem(p, RAW)]
        sem = raw_sem.at[lax.rem(p, RAW)]

        @pl.when(p < act_chunks)
        def _():
            at = pl.multiple_of(p * width, width)
            pltpu.make_async_copy(fac_act.at[pl.ds(at, width), :], slot, sem).start()

        @pl.when((p >= act_chunks) & (p < chunks))
        def _():
            at = pl.multiple_of((p - act_chunks) * width, width)
            pltpu.make_async_copy(fac_grad.at[pl.ds(at, width), :], slot, sem).start()

    for p in range(RAW):
        fetch(jnp.int32(p))

    barrier = pltpu.get_barrier_semaphore()
    friends = [(sibling, True), (ahead, has_ahead), (behind, has_behind)]
    if lines > 1:
        friends.append((across, True))
    for friend, there in friends:
        @pl.when(there)
        def _(friend=friend):
            pl.semaphore_signal(barrier, inc=1, device_id={"blk": friend}, device_id_type=MESH)
    ends_of_line = (place == 0).astype(jnp.int32) + (place == depth - 1).astype(jnp.int32)
    pl.semaphore_wait(barrier, len(friends) - ends_of_line)

    def swaps_first(c):
        return lax.rem(c, SWAP_FIRST[0]) == SWAP_FIRST[1]

    def sends(c, apart, side, same, act):
        at = place + side * apart
        ln = line if same else lines - 1 - line
        owner = block(at, ln, core)
        act(3, sibling, True, owner)
        along = True if same else swaps_first(c)
        if side <= 0:
            act(0, ahead, has_ahead & along, owner)
        if side >= 0:
            act(1, behind, has_behind & along, owner)
        if same and lines > 1:
            act(2, across, True if apart == 0 else jnp.logical_not(swaps_first(c)), owner)

    hops = []
    for same in ((True, False) if lines > 1 else (True,)):
        for apart in range(depth):
            for side in ((0,) if apart == 0 else (-1, 1)):
                hops.append((apart + (0 if same else 1), apart, side, same))
    hops.sort(key=lambda hop: hop[0])
    last_hop = depth - 1 + (1 if lines > 1 else 0) + 1

    def in_reach(apart, side):
        if side == 0:
            return True
        return (place >= apart) if side < 0 else (place + apart < depth)

    def forward(s):
        for hop, apart, side, same in hops:
            c = s - LAG * hop

            @pl.when((c >= 0) & (c < chunks) & in_reach(apart, side))
            def _(hop=hop, apart=apart, side=side, same=same, c=c):
                owner = block(place + side * apart, line if same else lines - 1 - line, core)
                if hop == 0:
                    pltpu.make_async_copy(
                        tok_act.at[:, pl.ds(0, width)], piece(c, me), load_sem.at[c]
                    ).wait()
                else:
                    arrived(c, owner)

                def act(link, target, when, owner):
                    @pl.when(when)
                    def _():
                        copy(link, c, owner, target).start()

                sends(c, apart, side, same, act)

    def drain(c):
        for hop, apart, side, same in hops:
            @pl.when(in_reach(apart, side))
            def _(apart=apart, side=side, same=same):
                def act(link, target, when, owner):
                    @pl.when(when)
                    def _():
                        copy(link, c, owner, target).wait_send()

                sends(c, apart, side, same, act)

    parts = eig_act.shape[0]
    for ref, first, n in ((eig_act, 0, parts), (eig_grad, parts, eig_grad.shape[0])):
        eigen = ref[...]
        damping = 0.1 * (jnp.sum(eigen, keepdims=True) / (n * 128))
        recip[pl.ds(first, n), :] = 1.0 / (eigen + damping)
    acc[...] = jnp.zeros_like(acc)
    columns = raw.shape[2]
    per_chunk = width // 128

    def precondition(p):
        slot = lax.rem(p, RAW)
        pltpu.make_async_copy(
            fac_act.at[pl.ds(0, width), :], raw.at[slot], raw_sem.at[slot]
        ).wait()

        def body(i, _):
            at = pl.multiple_of(i * 128, 128)
            row = recip[pl.ds(p * per_chunk + i, 1), :]
            scale = jnp.broadcast_to(row, (128, 128)).T
            for left in range(0, columns, 128):
                n = min(128, columns - left)
                part = raw[slot, pl.ds(at, 128), pl.ds(left, n)].astype(jnp.float32)
                pre[p % 2, pl.ds(at, 128), pl.ds(left, n)] = (part * scale[:, :n]).astype(jnp.bfloat16)
            return 0

        lax.fori_loop(0, per_chunk, body, 0)
        fetch(p + RAW)

    def multiply(c):
        for at in range(depth):
            for ln in range(lines):
                arrived(c, block(at, ln, 1 - core))
        which = (c >= act_chunks).astype(jnp.int32)
        acc[which] += jnp.dot(gat[c], pre[c % 2], preferred_element_type=jnp.float32)

    def step(s, _):
        forward(s)
        p = s - LAG * last_hop + 1

        @pl.when((p >= 0) & (p < chunks))
        def _():
            precondition(p)

        c = s - LAG * last_hop

        @pl.when(c >= 0)
        def _():
            multiply(c)

        return 0

    lax.fori_loop(0, chunks + LAG * last_hop, step, 0)

    docs = lengths.shape[1]
    queries = columns // RANK
    lens = jnp.broadcast_to(lengths[...].astype(jnp.float32), (docs, docs))
    down = lax.broadcasted_iota(jnp.int32, (docs, docs), 0)
    over = lax.broadcasted_iota(jnp.int32, (docs, docs), 1)
    ends = jnp.sum(jnp.where(over <= down, lens, 0.0), axis=1, keepdims=True)
    starts = jnp.sum(jnp.where(over < down, lens, 0.0), axis=1, keepdims=True)
    index = lax.broadcasted_iota(jnp.int32, (docs, tokens), 1).astype(jnp.float32)
    member = jnp.where((index >= starts) & (index < ends), 1.0, 0.0)
    product = acc[0] * acc[1]
    by_doc = jnp.dot(
        member, product, precision=lax.Precision.HIGHEST, preferred_element_type=jnp.float32
    )
    query = lax.broadcasted_iota(jnp.int32, (queries, columns), 0)
    column = lax.broadcasted_iota(jnp.int32, (queries, columns), 1)
    chosen = jnp.where((column >= query * RANK) & (column < query * RANK + RANK), 1.0, 0.0)
    out[...] = lax.dot_general(
        chosen, by_doc, (((1,), (1,)), ((), ())),
        precision=lax.Precision.HIGHEST, preferred_element_type=jnp.float32,
    )

    def drain_step(c, _):
        drain(c)
        return 0

    lax.fori_loop(0, chunks, drain_step, 0)


def local(lines, count, tok_act, tok_grad, fac_act, fac_grad, eig_act, eig_grad, lengths):
    rows, din = tok_act.shape
    dout = tok_grad.shape[1]
    columns = fac_act.shape[1]
    docs = lengths.shape[0]
    chunks = (din + dout) // CHUNK
    tokens = rows * count
    anywhere = pl.BlockSpec(memory_space=pl.ANY)
    vmem = pl.BlockSpec(memory_space=pltpu.VMEM)
    return pl.pallas_call(
        functools.partial(kernel, lines),
        out_shape=jax.ShapeDtypeStruct((columns // RANK, docs), jnp.float32),
        in_specs=[anywhere] * 4 + [vmem] * 3,
        out_specs=vmem,
        scratch_shapes=[
            pltpu.VMEM((chunks, tokens, CHUNK), jnp.bfloat16),
            pltpu.VMEM((RAW, CHUNK, columns), jnp.bfloat16),
            pltpu.VMEM((2, CHUNK, columns), jnp.bfloat16),
            pltpu.VMEM(((din + dout) // 128, 128), jnp.float32),
            pltpu.VMEM((2, tokens, columns), jnp.float32),
            pltpu.SemaphoreType.DMA((chunks,)),
            pltpu.SemaphoreType.DMA((RAW,)),
            pltpu.SemaphoreType.DMA((chunks, count)),
            pltpu.SemaphoreType.DMA((4, chunks, count // 2)),
        ],
        compiler_params=pltpu.CompilerParams(
            collective_id=0, has_side_effects=True, vmem_limit_bytes=60 * 2**20
        ),
    )(
        tok_act, tok_grad, fac_act, fac_grad,
        eig_act.reshape(-1, 128), eig_grad.reshape(-1, 128), lengths.reshape(1, docs),
    )


def solution(mesh):
    placed = (
        P(("grp", "blk"), None),
        P(("grp", "blk"), None),
        P(None, ("grp", "blk")),
        P(None, ("grp", "blk")),
        P(),
        P(),
        P("grp"),
    )
    count = mesh.shape["blk"]
    lines = 2 if count == 16 else 1
    return jax.shard_map(
        functools.partial(local, lines, count),
        mesh=mesh, in_specs=placed, out_specs=P(("grp", "blk"), None), check_vma=False,
    )
```

time: 457 us -> 143 us (0.31)
  waiting for transfers between devices: 271 us -> 0 us
  matrix products: 125 us -> 0 us
  Pallas kernels: 0 us -> 118 us
  other arithmetic: 16.4 us -> 0 us
  local copies, waits for them, and re-layouts: 35.4 us -> 24 us
  starting transfers between devices: 4.73 us -> 0 us
    ppermute x30 -> x0, waiting for transfers between devices: 271 us -> none  [from_behind(): return lax.ppermute(value, axis, pairs)]
    dot_general x48 -> x0, matrix products: 125 us -> none  [the longest x16 112 us: accumulate(): grad_proj = jnp.dot(grad_rows, grad_pre, preferred_element_type=jnp.float32)]
    pallas_call x0 -> x1, Pallas kernels: none -> 118 us  [local(): pl.pallas_call(functools.partial(kernel, lines), out_shape=jax.ShapeDtype...]
    convert_element_type x2 -> x0, other arithmetic: 11.8 us -> none  [precondition(): (factors.astype(jnp.float32) / (eigen + damping)[:, None]).astype(jnp.bfl...]
    unnamed x14 -> x3, local copies, waits for them, and re-layouts: 32.6 us -> 24 us
    ppermute x30 -> x0, starting transfers between devices: 4.73 us -> none  [from_behind(): return lax.ppermute(value, axis, pairs)]
  transfers between devices with their start and end apart: 30 -> 0, of which waited for: 15 -> 0; matrix products, arithmetic and copies ran while one was open for 0% -> 0% of each run, Pallas kernels for 0% -> 0%
where the time goes in v1:
time: 143 us; the launch traced here: 142 us
  Pallas kernels  118 us (83%)
  local copies, waits for them, and re-layouts  24 us (17%)
    pallas_call x1, Pallas kernels, local(): pl.pallas_call(functools.partial(kernel, lines), out_shape=jax.ShapeDtype...  118 us
    unnamed x3, local copies, waits for them, and re-layouts  24 us

profile of v1, /device:TPU:0, one launch (start us, length us, event | category | flops | bytes accessed | tf_op | source)
XLA Modules:
  0.0 142.1 jit_solution(811220673892785597)
XLA Ops:
  0.0 6.0 %copy.8.fac_act = bf16[8192,192]{1,0:T(8,128)(2,1)} copy(bf16[8192,192]{0,1:T(8,128)(2,1)} %param.9) | data formatting | bytes 6291456 | tf_op args[2]
  6.0 16.7 %copy.9.fac_grad = bf16[28672,192]{1,0:T(8,128)(2,1)} copy(bf16[28672,192]{0,1:T(8,128)(2,1)} %param.10) | data formatting | bytes 22020096 | tf_op args[3]
  22.7 118.1 %shard_map.73 = f32[6,16]{1,0:T(8,128)} custom-call(bf16[16,8192]{1,0:T(8,128)(2,1)} %tok_act.1, bf16[16,28672]{1,0:T(8,128)(2,1)} %tok_grad.1, bf16[8192,192]{1,0:T(8,128)(2,1)} %copy.8.fac_act, bf16[28672,192]{1,0:T(8,128)(2,1)} %copy.9.fac_grad, f32[64,128]{1,0:T(8,128)} %bitcast.4, f32[224,128]{1,0:T(8,128)} %bitcast.3, s32[1,16]{1,0:T(1,128)} %bitcast.5), custom_call_target="tpu_custom_call" | custom-call | tf_op jit(solution)/shard_map/pallas_call | solution.py:239
  140.8 1.3 copy.11

commit v2 on v1

--- a/solution.py
+++ b/solution.py
@@ -8,9 +8,9 @@
 from jax.sharding import PartitionSpec as P
 
 RANK = 32
-CHUNK = 2048
+CHUNK = 4096
 LAG = 1
-SWAP_FIRST = (6, 3)
+SWAP_FIRST = (5, 2)
 RAW = 3
 MESH = pl.DeviceIdType.MESH
 
@@ -64,12 +64,12 @@
         @pl.when(p < act_chunks)
         def _():
             at = pl.multiple_of(p * width, width)
-            pltpu.make_async_copy(fac_act.at[pl.ds(at, width), :], slot, sem).start()
+            pltpu.make_async_copy(fac_act.at[:, pl.ds(at, width)], slot, sem).start()
 
         @pl.when((p >= act_chunks) & (p < chunks))
         def _():
             at = pl.multiple_of((p - act_chunks) * width, width)
-            pltpu.make_async_copy(fac_grad.at[pl.ds(at, width), :], slot, sem).start()
+            pltpu.make_async_copy(fac_grad.at[:, pl.ds(at, width)], slot, sem).start()
 
     for p in range(RAW):
         fetch(jnp.int32(p))
@@ -152,23 +152,20 @@
         damping = 0.1 * (jnp.sum(eigen, keepdims=True) / (n * 128))
         recip[pl.ds(first, n), :] = 1.0 / (eigen + damping)
     acc[...] = jnp.zeros_like(acc)
-    columns = raw.shape[2]
+    columns = raw.shape[1]
     per_chunk = width // 128
 
     def precondition(p):
         slot = lax.rem(p, RAW)
         pltpu.make_async_copy(
-            fac_act.at[pl.ds(0, width), :], raw.at[slot], raw_sem.at[slot]
+            fac_act.at[:, pl.ds(0, width)], raw.at[slot], raw_sem.at[slot]
         ).wait()
 
         def body(i, _):
             at = pl.multiple_of(i * 128, 128)
             row = recip[pl.ds(p * per_chunk + i, 1), :]
-            scale = jnp.broadcast_to(row, (128, 128)).T
-            for left in range(0, columns, 128):
-                n = min(128, columns - left)
-                part = raw[slot, pl.ds(at, 128), pl.ds(left, n)].astype(jnp.float32)
-                pre[p % 2, pl.ds(at, 128), pl.ds(left, n)] = (part * scale[:, :n]).astype(jnp.bfloat16)
+            part = raw[slot, :, pl.ds(at, 128)].astype(jnp.float32)
+            pre[p % 2, :, pl.ds(at, 128)] = (part * row).astype(jnp.bfloat16)
             return 0
 
         lax.fori_loop(0, per_chunk, body, 0)
@@ -179,7 +176,9 @@
             for ln in range(lines):
                 arrived(c, block(at, ln, 1 - core))
         which = (c >= act_chunks).astype(jnp.int32)
-        acc[which] += jnp.dot(gat[c], pre[c % 2], preferred_element_type=jnp.float32)
+        acc[which] += lax.dot_general(
+            gat[c], pre[c % 2], (((1,), (1,)), ((), ())), preferred_element_type=jnp.float32
+        )
 
     def step(s, _):
         forward(s)
@@ -228,9 +227,10 @@
 
 
 def local(lines, count, tok_act, tok_grad, fac_act, fac_grad, eig_act, eig_grad, lengths):
+    fac_act, fac_grad = fac_act.T, fac_grad.T
     rows, din = tok_act.shape
     dout = tok_grad.shape[1]
-    columns = fac_act.shape[1]
+    columns = fac_act.shape[0]
     docs = lengths.shape[0]
     chunks = (din + dout) // CHUNK
     tokens = rows * count
@@ -243,8 +243,8 @@
         out_specs=vmem,
         scratch_shapes=[
             pltpu.VMEM((chunks, tokens, CHUNK), jnp.bfloat16),
-            pltpu.VMEM((RAW, CHUNK, columns), jnp.bfloat16),
-            pltpu.VMEM((2, CHUNK, columns), jnp.bfloat16),
+            pltpu.VMEM((RAW, columns, CHUNK), jnp.bfloat16),
+            pltpu.VMEM((2, columns, CHUNK), jnp.bfloat16),
             pltpu.VMEM(((din + dout) // 128, 128), jnp.float32),
             pltpu.VMEM((2, tokens, columns), jnp.float32),
             pltpu.SemaphoreType.DMA((chunks,)),

time: 143 us -> 112 us (0.78)
  local copies, waits for them, and re-layouts: 24 us -> 1.28 us
  Pallas kernels: 118 us -> 110 us
    unnamed x3 -> x1, local copies, waits for them, and re-layouts: 24 us -> 1.28 us
    pallas_call x1, Pallas kernels: 118 us -> 110 us  [local(): pl.pallas_call(functools.partial(kernel, lines), out_shape=jax.ShapeDtype...]
where the time goes in v2:
time: 112 us
  Pallas kernels  110 us (98%)
  local copies, waits for them, and re-layouts  1.28 us (1%)
    pallas_call x1, Pallas kernels, local(): pl.pallas_call(functools.partial(kernel, lines), out_shape=jax.ShapeDtype...  110 us

profile of v2, /device:TPU:0, one launch (start us, length us, event | category | flops | bytes accessed | tf_op | source)
XLA Modules:
  0.0 111.7 jit_solution(10633992935733581606)
XLA Ops:
  0.0 110.4 %shard_map.73 = f32[6,16]{1,0:T(8,128)} custom-call(bf16[16,8192]{1,0:T(8,128)(2,1)} %tok_act.1, bf16[16,28672]{1,0:T(8,128)(2,1)} %tok_grad.1, bf16[192,8192]{1,0:T(8,128)(2,1)} %bitcast.6, bf16[192,28672]{1,0:T(8,128)(2,1)} %bitcast.5, f32[64,128]{1,0:T(8,128)} %bitcast.8, f32[224,128]{1,0:T(8,128)} %bitcast.7, s32[1,16]{1,0:T(1,128)} %bitcast.9), custom_call_target="tpu_custom_call" | custom-call | tf_op jit(solution)/shard_map/pallas_call | solution.py:239
  110.4 1.3 %copy.9 = f32[6,16]{1,0:T(8,128)} copy(f32[6,16]{1,0:T(8,128)} %shard_map.73) | data formatting | bytes 768

commit v3 on v2

--- a/solution.py
+++ b/solution.py
@@ -10,7 +10,7 @@
 RANK = 32
 CHUNK = 4096
 LAG = 1
-SWAP_FIRST = (5, 2)
+SWAP_FIRST = (6, 1, 0)
 RAW = 3
 MESH = pl.DeviceIdType.MESH
 
@@ -85,21 +85,21 @@
     ends_of_line = (place == 0).astype(jnp.int32) + (place == depth - 1).astype(jnp.int32)
     pl.semaphore_wait(barrier, len(friends) - ends_of_line)
 
-    def swaps_first(c):
-        return lax.rem(c, SWAP_FIRST[0]) == SWAP_FIRST[1]
+    def swaps_first(c, at):
+        return lax.rem(c + SWAP_FIRST[1] * (at + depth * core), SWAP_FIRST[0]) == SWAP_FIRST[2]
 
     def sends(c, apart, side, same, act):
         at = place + side * apart
         ln = line if same else lines - 1 - line
         owner = block(at, ln, core)
-        act(3, sibling, True, owner)
-        along = True if same else swaps_first(c)
+        along = True if same else swaps_first(c, at)
         if side <= 0:
             act(0, ahead, has_ahead & along, owner)
         if side >= 0:
             act(1, behind, has_behind & along, owner)
         if same and lines > 1:
-            act(2, across, True if apart == 0 else jnp.logical_not(swaps_first(c)), owner)
+            act(2, across, True if apart == 0 else jnp.logical_not(swaps_first(c, at)), owner)
+        act(3, sibling, True, owner)
 
     hops = []
     for same in ((True, False) if lines > 1 else (True,)):

time: 112 us -> 109 us (0.973)
  Pallas kernels: 110 us -> 108 us
    pallas_call x1, Pallas kernels: 110 us -> 108 us  [local(): pl.pallas_call(functools.partial(kernel, lines), out_shape=jax.ShapeDtype...]
where the time goes in v3:
time: 109 us
  Pallas kernels  108 us (99%)
  local copies, waits for them, and re-layouts  1.28 us (1%)
    pallas_call x1, Pallas kernels, local(): pl.pallas_call(functools.partial(kernel, lines), out_shape=jax.ShapeDtype...  108 us

profile of v3, /device:TPU:0, one launch (start us, length us, event | category | flops | bytes accessed | tf_op | source)
XLA Modules:
  0.0 108.9 jit_solution(17263800227657994495)
XLA Ops:
  0.0 107.6 %shard_map.73 = f32[6,16]{1,0:T(8,128)} custom-call(bf16[16,8192]{1,0:T(8,128)(2,1)} %tok_act.1, bf16[16,28672]{1,0:T(8,128)(2,1)} %tok_grad.1, bf16[192,8192]{1,0:T(8,128)(2,1)} %bitcast.6, bf16[192,28672]{1,0:T(8,128)(2,1)} %bitcast.5, f32[64,128]{1,0:T(8,128)} %bitcast.8, f32[224,128]{1,0:T(8,128)} %bitcast.7, s32[1,16]{1,0:T(1,128)} %bitcast.9), custom_call_target="tpu_custom_call" | custom-call | tf_op jit(solution)/shard_map/pallas_call | solution.py:239
  107.6 1.3 %copy.9 = f32[6,16]{1,0:T(8,128)} copy(f32[6,16]{1,0:T(8,128)} %shard_map.73) | data formatting | bytes 768
